TPU v7x, 128 devices: a whole 4x4x4 slice. The times are simulated.
128 devices in a mesh: session: 8 (over y, core), item: 16 (over x, z).
Axes of the slice: x: 4, y: 4, z: 4, core: 2. Of those that a mesh axis runs over, the one named last changes fastest.
Arguments:
- cache: bfloat16 [32, 4096, 2, 512], P('session', 'item'), may hold values from -6 to 6
- lengths: int32 [32], P('session'), may hold values from 512 to 4096
- new_slot: int32 [32], P('session'), may hold values from 0 to 31, as said below
- unique_ids: int32 [8, 5120], P('session', 'item'), may hold values from 0 to 1048575, as said below
- inverse: int32 [32, 4096], P('session', 'item'), may hold values from 0 to 319, as said below
- table: bfloat16 [1048576, 512], P(('session', 'item')), may hold values from -6 to 6
- w_qu: bfloat16 [512, 1024], replicated, may hold values from -0.25 to 0.25
- w_out: bfloat16 [512, 512], replicated, may hold values from -0.25 to 0.25
- w_head: bfloat16 [512], replicated, may hold values from -0.25 to 0.25
Outputs:
- migrated_cache: bfloat16 [32, 4096, 2, 512], P('session', 'item')
- scores: float32 [32, 4096], P('session', 'item')
Inputs may be any that keep to these rules, and one draw needn't show every extreme that they name: `new_slot`: A permutation of the session slots; the owner of slot g is g // 4; no two sessions of one owner move to the same owner. `unique_ids`: each device's block of 320 entries holds distinct ids; id v lives on device v // 8192 of session+item. In every block each device is named 1 to 4 times, each of these four counts by a quarter of the devices. `inverse`: indexes the same device's block of unique_ids; every entry of a block is used.
All inputs are finite; a program needn't handle non-finite values.
Results may differ from a plain program's by a relative error of at most 0.003.
Values may be sent and summed in bfloat16 or wider, within the bound.
A program may use at most 192 MiB of HBM per device.

v0:
```python
import math

import jax
import jax.numpy as jnp
from jax import lax
from jax.sharding import PartitionSpec as P

HEADS = 4
QCAP = 4


def attend_block(queries, group, first, lens):
    rows, sessions, width = queries.shape
    span = group.shape[1]
    size = width // HEADS
    query_heads = queries.reshape(rows, sessions, HEADS, size)
    keys = group[:, :, 0, :].reshape(sessions, span, HEADS, size)
    values = group[:, :, 1, :].reshape(sessions, span, HEADS, size)
    logits = jnp.einsum(
        "rshd,sehd->shre", query_heads, keys, preferred_element_type=jnp.float32
    ) * (1.0 / math.sqrt(size))
    position = first + jnp.arange(span, dtype=jnp.int32)
    live = position[None, :] < lens[:, None]
    weights = jnp.where(live[:, None, None, :], jax.nn.silu(logits), 0.0).astype(jnp.bfloat16)
    mixed = jnp.einsum("shre,sehd->rshd", weights, values, preferred_element_type=jnp.float32)
    return mixed.reshape(rows, sessions, width)


def attend(queries, group, first, lens):
    rows, sessions, width = queries.shape
    span = group.shape[1]
    row_block = 512
    turns = span // span

    def one_rows(block):

        def step(total, index):
            return (total + attend_block(block, group, first + index * span, lens), None)

        start = jnp.zeros((block.shape[0], sessions, width), jnp.float32)
        total, _ = lax.scan(step, start, jnp.arange(turns, dtype=jnp.int32))
        return total

    blocks = queries.reshape(rows // row_block, row_block, sessions, width)
    return lax.map(one_rows, blocks).reshape(rows, sessions, width)


def per_device(cache, lengths, new_slot, unique_ids, inverse, table, w_qu, w_out, w_head):
    sessions = cache.shape[0]
    events = cache.shape[1]
    width = cache.shape[3]
    owners = lax.axis_size("session")
    all_slots, all_lengths = (
        lax.all_gather(new_slot, "session", axis=0, tiled=True),
        lax.all_gather(lengths, "session", axis=0, tiled=True),
    )
    total = all_slots.shape[0]
    here = lax.axis_index("session")
    my_slots = here * sessions + jnp.arange(sessions, dtype=jnp.int32)
    found = all_slots[None, :] == my_slots[:, None]
    anchor = jnp.sum(jnp.where(found, jnp.arange(total, dtype=jnp.int32)[None, :], 0), axis=1)
    source = anchor // sessions
    new_lengths = jnp.sum(jnp.where(found, all_lengths[None, :], 0), axis=1)
    target = new_slot // sessions
    chosen = target[None, :] == jnp.arange(owners, dtype=jnp.int32)[:, None]
    which = jnp.sum(jnp.where(chosen, jnp.arange(sessions, dtype=jnp.int32)[None, :], 0), axis=1)
    present = jnp.any(chosen, axis=1)
    outgoing = jnp.where(
        present[:, None, None, None], jnp.take(cache, which, axis=0), jnp.zeros((), cache.dtype)
    )
    incoming = lax.all_to_all(outgoing, "session", split_axis=0, concat_axis=0, tiled=True)
    migrated = jnp.take(incoming, source, axis=0)
    ids = unique_ids[0]
    items = table.shape[0]
    peers = lax.axis_size(("session", "item"))
    holder = ids // items
    row_ids = ids % items
    member = (holder[:, None] == jnp.arange(peers, dtype=jnp.int32)[None, :]).astype(jnp.int32)
    rank = jnp.sum(jnp.cumsum(member, axis=0) * member, axis=1) - 1
    place = holder * QCAP + rank
    requests = jnp.zeros((peers * QCAP,), jnp.int32).at[place].set(row_ids).reshape(peers, QCAP)
    fetched = lax.all_to_all(
        jnp.take(
            table,
            lax.all_to_all(requests, ("session", "item"), split_axis=0, concat_axis=0, tiled=True),
            axis=0,
        ),
        ("session", "item"),
        split_axis=0,
        concat_axis=0,
        tiled=True,
    ).reshape(peers * QCAP, width)
    unique_rows = jnp.take(fetched, place, axis=0)
    candidates = jnp.take(unique_rows, inverse.T, axis=0)
    count = candidates.shape[0]
    flat = candidates.reshape(count * sessions, width)
    projected = jnp.dot(flat, w_qu, preferred_element_type=jnp.float32)
    queries = projected[:, :width].astype(jnp.bfloat16).reshape(count, sessions, width)
    gate = jax.nn.silu(projected[:, width:])
    everyone = lax.all_gather(queries, "item", axis=0, tiled=True)
    first = lax.axis_index("item") * events
    mixed = lax.psum_scatter(
        attend(everyone, migrated, first, new_lengths), "item", scatter_dimension=0, tiled=True
    )
    mixed = mixed.reshape(count * sessions, width)
    normed = mixed * lax.rsqrt(jnp.mean(mixed * mixed, axis=-1, keepdims=True) + 1e-06)
    gated = (normed * gate).astype(jnp.bfloat16)
    hidden = flat.astype(jnp.float32) + jnp.dot(gated, w_out, preferred_element_type=jnp.float32)
    scores = (
        jnp.sum(hidden * w_head.astype(jnp.float32)[None, :], axis=1).reshape(count, sessions).T
    )
    return (migrated, scores)


def solution(mesh):
    placed = (
        P("session", "item", None, None),
        P("session"),
        P("session"),
        P("session", "item"),
        P("session", "item"),
        P(("session", "item"), None),
        P(),
        P(),
        P(),
    )
    return jax.shard_map(
        per_device,
        mesh=mesh,
        in_specs=placed,
        out_specs=(P("session", "item", None, None), P("session", "item")),
        check_vma=False,
    )
```

profile of v0, /device:TPU:0, one launch (start us, length us, event | category | flops | bytes accessed | tf_op | source)
XLA Modules:
  0.0 591.2 jit_solution(7166826389696691697)
XLA Ops:
  9.4 2.9 scatter_custom_fusion
  13.0 11.1 %all-to-all-start.1 = ((s32[128,1,4]{2,1,0:T(1,128)}), s32[128,1,4]{2,1,0:T(1,128)S(1)}, u32[]{:S(2)}, u32[]{:S(2)}) async-start(s32[128,1,4]{2,1,0:T(1,128)} %bitcast.16), calls=%async_computation.1 | async-start | bytes 131072 | tf_op jit(solution)/shard_map/all_to_all | solution.py:85
  26.2 7.4 %all-to-all-done.1 = s32[128,1,4]{2,1,0:T(1,128)S(1)} async-done(((s32[128,1,4]{2,1,0:T(1,128)}), s32[128,1,4]{2,1,0:T(1,128)S(1)}, u32[]{:S(2)}, u32[]{:S(2)}) %all-to-all-start.1) | async-done | bytes 2080 | tf_op jit(solution)/shard_map/all_to_all | solution.py:85
  33.7 6.4 %gather_fusion.2 = bf16[512,512]{1,0:T(8,128)(2,1)S(1)} fusion(bf16[8192,512]{1,0:T(8,128)(2,1)} %param.16, s32[1024]{0:T(1024)S(1)} %pad_clamp_fusion.1), kind=kCustom, calls=%fused_computation.2 | custom fusion | bytes 1050624 | tf_op jit(solution)/shard_map/jit(_take)/gather | solution.py:83
  41.5 4.6 all-to-all-start.2
  46.4 13.3 %all-to-all-done.2 = bf16[128,4,512]{2,1,0:T(4,128)(2,1)S(1)} async-done(((bf16[128,4,512]{2,1,0:T(4,128)(2,1)}), bf16[128,4,512]{2,1,0:T(4,128)(2,1)S(1)}, u32[]{:S(2)}, u32[]{:S(2)}) %all-to-all-start.2) | async-done | bytes 524320 | tf_op jit(solution)/shard_map/all_to_all | solution.py:82
  62.0 5.1 gather_fusion.4
  68.6 2.9 fusion.6
  79.3 9.8 %gather_fusion = bf16[8,256,2,512]{3,2,1,0:T(2,128)(2,1)} fusion(bf16[4,256,2,512]{3,2,1,0:T(2,128)(2,1)S(1)} %copy-done, s32[1024]{0:T(1024)S(1)} %pad_clamp_fusion.3), kind=kCustom, calls=%fused_computation | custom fusion | bytes 8388640 | tf_op jit(solution)/shard_map/jit(_take)/gather | solution.py:69
  89.2 8.1 %broadcast_select_fusion.1 = bf16[8,256,2,512]{3,2,1,0:T(2,128)(2,1)} fusion(pred[8]{0:T(512)(128)(4,1)S(1)} %fusion.13, bf16[8,256,2,512]{3,2,1,0:T(2,128)(2,1)} %gather_fusion, pred[8]{0:T(512)(128)(4,1)S(1)} %compare_and_fusion.3), kind=kLoop, calls=%fused_computation.17 | loop fusion | flops 4194304 | bytes 8388624 | tf_op jit(solution)/shard_map/jit(_where)/select_n | solution.py:68
  97.4 4.7 all-to-all-start
  103.9 50.6 %all-reduce.3 = (s32[32]{0:T(128)S(1)}, s32[32]{0:T(128)S(1)}) all-reduce(s32[32]{0:T(128)S(1)} %dynamic-update-slice.1, s32[32]{0:T(128)S(1)} %dynamic-update-slice), channel_id=1, replica_groups=mesh['session'=8,'item'=16] {'session'}, use_global_device_ids=true, to_apply=%add.2 | all-reduce | flops 64 | bytes 512
  154.7 5.1 copy.59
  159.8 4.4 gather_fusion.1
  168.9 17.6 %all-gather.2.cloned.1.call-done = bf16[4096,4,512]{2,0,1:T(8,128)(2,1)} async-done(((bf16[256,4,512]{2,0,1:T(8,128)(2,1)}), bf16[4096,4,512]{2,0,1:T(8,128)(2,1)}) %all-gather.2.cloned.1.call-update) | async-done | bytes 16777232 | tf_op jit(solution)/shard_map/all_gather | solution.py:100
  186.5 190.5 %while.17 = (s32[]{:T(128)}, f32[8,512,4,512]{3,1,0,2:T(8,128)}, s32[]{:T(128)}, s32[4]{0:T(128)S(1)}, bf16[8,512,4,512]{3,1,0,2:T(8,128)(2,1)}, /*index=5*/bf16[4,256,2,512]{1,3,0,2:T(8,128)(2,1)}, s32[]{:T(128)}) while((s32[]{:T(128)}, f32[8,512,4,512]{3,1,0,2:T(8,128)}, s32[]{:T(128)}, s32[4]{0:T(128)S(1)}, ...), condition=%wide.region_9.10_spmd, body=%wide.region_8.9_spmd.sunk | while | flops 1088423168 | bytes 46142080 | solution.py:45
  190.6 2.8 fusion.36
  193.5 7.0 %fusion.37 = f32[4,4,512,128]{2,3,1,0:T(8,128)} fusion(bf16[4,256,4,128]{1,3,2,0:T(8,128)(2,1)} %bitcast.75, pred[4,256]{1,0:T(4,128)(4,1)S(1)} %broadcast_compare_fusion.3, bf16[512,4,4,128]{0,3,2,1:T(8,128)(2,1)S(1)} %bitcast.72, bf16[4,256,4,128]{1,3,2,0:T(8,128)(2,1)S(1)} %bitcast.74), kind=kOutput, calls=%fused_computation.7.clone.1 | convolution fusion | flops 1088421888 | bytes 8389632 | tf_op jit(solution)/shard_map/while/body/eval_jaxpr/while/body/eval_jaxpr/shre,sehd->rshd/dot_general | solution.py:25
  200.5 5.2 copy.86
  205.7 4.7 constant_dynamic-update-slice_fusion.2
  214.5 2.8 fusion.36
  217.4 7.0 %fusion.37 = f32[4,4,512,128]{2,3,1,0:T(8,128)} fusion(bf16[4,256,4,128]{1,3,2,0:T(8,128)(2,1)} %bitcast.75, pred[4,256]{1,0:T(4,128)(4,1)S(1)} %broadcast_compare_fusion.3, bf16[512,4,4,128]{0,3,2,1:T(8,128)(2,1)S(1)} %bitcast.72, bf16[4,256,4,128]{1,3,2,0:T(8,128)(2,1)S(1)} %bitcast.74), kind=kOutput, calls=%fused_computation.7.clone.1 | convolution fusion | flops 1088421888 | bytes 8389632 | tf_op jit(solution)/shard_map/while/body/eval_jaxpr/while/body/eval_jaxpr/shre,sehd->rshd/dot_general | solution.py:25
  224.4 5.2 copy.86
  229.6 4.6 constant_dynamic-update-slice_fusion.2
  238.3 2.8 fusion.36
  241.2 7.0 %fusion.37 = f32[4,4,512,128]{2,3,1,0:T(8,128)} fusion(bf16[4,256,4,128]{1,3,2,0:T(8,128)(2,1)} %bitcast.75, pred[4,256]{1,0:T(4,128)(4,1)S(1)} %broadcast_compare_fusion.3, bf16[512,4,4,128]{0,3,2,1:T(8,128)(2,1)S(1)} %bitcast.72, bf16[4,256,4,128]{1,3,2,0:T(8,128)(2,1)S(1)} %bitcast.74), kind=kOutput, calls=%fused_computation.7.clone.1 | convolution fusion | flops 1088421888 | bytes 8389632 | tf_op jit(solution)/shard_map/while/body/eval_jaxpr/while/body/eval_jaxpr/shre,sehd->rshd/dot_general | solution.py:25
  248.2 5.2 copy.86
  253.4 4.6 constant_dynamic-update-slice_fusion.2
  265.0 7.0 %fusion.37 = f32[4,4,512,128]{2,3,1,0:T(8,128)} fusion(bf16[4,256,4,128]{1,3,2,0:T(8,128)(2,1)} %bitcast.75, pred[4,256]{1,0:T(4,128)(4,1)S(1)} %broadcast_compare_fusion.3, bf16[512,4,4,128]{0,3,2,1:T(8,128)(2,1)S(1)} %bitcast.72, bf16[4,256,4,128]{1,3,2,0:T(8,128)(2,1)S(1)} %bitcast.74), kind=kOutput, calls=%fused_computation.7.clone.1 | convolution fusion | flops 1088421888 | bytes 8389632 | tf_op jit(solution)/shard_map/while/body/eval_jaxpr/while/body/eval_jaxpr/shre,sehd->rshd/dot_general | solution.py:25
  272.0 5.2 copy.86
  277.2 4.6 constant_dynamic-update-slice_fusion.2
  288.8 7.0 %fusion.37 = f32[4,4,512,128]{2,3,1,0:T(8,128)} fusion(bf16[4,256,4,128]{1,3,2,0:T(8,128)(2,1)} %bitcast.75, pred[4,256]{1,0:T(4,128)(4,1)S(1)} %broadcast_compare_fusion.3, bf16[512,4,4,128]{0,3,2,1:T(8,128)(2,1)S(1)} %bitcast.72, bf16[4,256,4,128]{1,3,2,0:T(8,128)(2,1)S(1)} %bitcast.74), kind=kOutput, calls=%fused_computation.7.clone.1 | convolution fusion | flops 1088421888 | bytes 8389632 | tf_op jit(solution)/shard_map/while/body/eval_jaxpr/while/body/eval_jaxpr/shre,sehd->rshd/dot_general | solution.py:25
  295.8 5.2 copy.86
  301.0 4.7 constant_dynamic-update-slice_fusion.2
  312.7 7.0 %fusion.37 = f32[4,4,512,128]{2,3,1,0:T(8,128)} fusion(bf16[4,256,4,128]{1,3,2,0:T(8,128)(2,1)} %bitcast.75, pred[4,256]{1,0:T(4,128)(4,1)S(1)} %broadcast_compare_fusion.3, bf16[512,4,4,128]{0,3,2,1:T(8,128)(2,1)S(1)} %bitcast.72, bf16[4,256,4,128]{1,3,2,0:T(8,128)(2,1)S(1)} %bitcast.74), kind=kOutput, calls=%fused_computation.7.clone.1 | convolution fusion | flops 1088421888 | bytes 8389632 | tf_op jit(solution)/shard_map/while/body/eval_jaxpr/while/body/eval_jaxpr/shre,sehd->rshd/dot_general | solution.py:25
  319.6 5.2 copy.86
  324.9 4.6 constant_dynamic-update-slice_fusion.2
  336.5 7.0 %fusion.37 = f32[4,4,512,128]{2,3,1,0:T(8,128)} fusion(bf16[4,256,4,128]{1,3,2,0:T(8,128)(2,1)} %bitcast.75, pred[4,256]{1,0:T(4,128)(4,1)S(1)} %broadcast_compare_fusion.3, bf16[512,4,4,128]{0,3,2,1:T(8,128)(2,1)S(1)} %bitcast.72, bf16[4,256,4,128]{1,3,2,0:T(8,128)(2,1)S(1)} %bitcast.74), kind=kOutput, calls=%fused_computation.7.clone.1 | convolution fusion | flops 1088421888 | bytes 8389632 | tf_op jit(solution)/shard_map/while/body/eval_jaxpr/while/body/eval_jaxpr/shre,sehd->rshd/dot_general | solution.py:25
  343.4 5.2 copy.86
  348.7 4.6 constant_dynamic-update-slice_fusion.2
  360.3 7.0 %fusion.37 = f32[4,4,512,128]{2,3,1,0:T(8,128)} fusion(bf16[4,256,4,128]{1,3,2,0:T(8,128)(2,1)} %bitcast.75, pred[4,256]{1,0:T(4,128)(4,1)S(1)} %broadcast_compare_fusion.3, bf16[512,4,4,128]{0,3,2,1:T(8,128)(2,1)S(1)} %bitcast.72, bf16[4,256,4,128]{1,3,2,0:T(8,128)(2,1)S(1)} %bitcast.74), kind=kOutput, calls=%fused_computation.7.clone.1 | convolution fusion | flops 1088421888 | bytes 8389632 | tf_op jit(solution)/shard_map/while/body/eval_jaxpr/while/body/eval_jaxpr/shre,sehd->rshd/dot_general | solution.py:25
  367.2 5.2 copy.86
  372.4 4.6 constant_dynamic-update-slice_fusion.2
  378.7 3.5 copy.72
  382.1 189.9 %reduce-scatter.2.cloned.1.call-done = f32[256,4,512]{2,0,1:T(8,128)} async-done(((f32[4096,4,512]{2,0,1:T(8,128)}), f32[256,4,512]{2,0,1:T(8,128)}) %reduce-scatter.2.cloned.1.call-update) | async-done | bytes 2097168 | tf_op jit(solution)/shard_map/reduce_scatter | solution.py:102
  572.0 4.4 copy.70
  576.4 3.1 reshape.342
  580.0 3.5 multiply_reduce_fusion
  (143 shorter events, 74.7 us)
Async XLA Ops:
  7.2 72.2 %copy-start = (bf16[4,256,2,512]{3,2,1,0:T(2,128)(2,1)S(1)}, bf16[4,256,2,512]{3,2,1,0:T(2,128)(2,1)}, u32[]{:S(2)}) copy-start(bf16[4,256,2,512]{3,2,1,0:T(2,128)(2,1)} %param.11) | copy-start | bytes 6291460
  13.0 20.6 %all-to-all-start.1 = ((s32[128,1,4]{2,1,0:T(1,128)}), s32[128,1,4]{2,1,0:T(1,128)S(1)}, u32[]{:S(2)}, u32[]{:S(2)}) async-start(s32[128,1,4]{2,1,0:T(1,128)} %bitcast.16), calls=%async_computation.1 | async-start | bytes 131072 | tf_op jit(solution)/shard_map/all_to_all | solution.py:85
  41.5 18.2 %all-to-all-start.2 = ((bf16[128,4,512]{2,1,0:T(4,128)(2,1)}), bf16[128,4,512]{2,1,0:T(4,128)(2,1)S(1)}, u32[]{:S(2)}, u32[]{:S(2)}) async-start(bf16[128,4,512]{2,1,0:T(4,128)(2,1)} %broadcast_select_fusion.5), calls=%async_computation.2 | async-start | bytes 1048576 | tf_op jit(solution)/shard_map/all_to_all | solution.py:82
  46.1 140.4 %all-gather.2.cloned.1.call-start = ((), (), s32[]{:S(2)}) async-start(), calls=%async_computation.4 | async-start | bytes 17825792 | tf_op jit(solution)/shard_map/all_gather | solution.py:100
  68.6 6.1 %copy-start.7 = (bf16[1024,512]{0,1:T(8,128)(2,1)}, bf16[1024,512]{0,1:T(8,128)(2,1)S(1)}, u32[]{:S(2)}) copy-start(bf16[1024,512]{0,1:T(8,128)(2,1)S(1)} %copy.65) | copy-start | bytes 3145732
  71.5 2.0 copy-start.5
  73.5 5.7 copy-start.10
  97.3 4.8 copy-start.12
  97.3 6.3 %copy-start.11 = (s32[4]{0:T(128)S(1)}, s32[4]{0:T(128)}, u32[]{:S(2)}) copy-start(s32[4]{0:T(128)} %param.12) | copy-start | bytes 52
  97.4 57.4 %all-to-all-start = ((bf16[8,256,2,512]{3,2,1,0:T(2,128)(2,1)}), bf16[8,256,2,512]{3,2,1,0:T(2,128)(2,1)}, u32[]{:S(2)}, u32[]{:S(2)}) async-start(bf16[8,256,2,512]{3,2,1,0:T(2,128)(2,1)} %broadcast_select_fusion.1), calls=%async_computation | async-start | bytes 8388608 | tf_op jit(solution)/shard_map/all_to_all | solution.py:71
  102.1 469.9 %reduce-scatter.2.cloned.1.call-start = ((), (), s32[]{:S(2)}) async-start(), calls=%async_computation.5 | async-start | bytes 35651584 | tf_op jit(solution)/shard_map/reduce_scatter | solution.py:102
  166.1 20.4 %copy-start.3 = (bf16[4,256,2,512]{3,1,2,0:T(8,128)(2,1)}, bf16[4,256,2,512]{3,1,2,0:T(8,128)(2,1)S(1)}, u32[]{:S(2)}) copy-start(bf16[4,256,2,512]{3,1,2,0:T(8,128)(2,1)S(1)} %broadcast_select_fusion.2) | copy-start | bytes 6291460
  190.6 2.9 copy-start.2
  214.5 2.9 copy-start.2
  238.3 2.9 copy-start.2
  262.1 2.9 copy-start.2
  285.9 2.9 copy-start.2
  309.8 2.9 copy-start.2
  333.6 2.9 copy-start.2
  357.4 2.9 copy-start.2
  377.1 0.7 copy-start.9
  377.1 1.6 copy-start.4
  572.0 7.5 %copy-start.6 = (f32[256,4,512]{2,0,1:T(8,128)S(1)}, f32[256,4,512]{2,0,1:T(8,128)}, u32[]{:S(2)}) copy-start(f32[256,4,512]{2,0,1:T(8,128)} %reduce-scatter.2.cloned.1.call-done) | copy-start | bytes 6291460
  576.4 3.6 copy-start.8
  579.9 4.5 copy-start.1
Sparse Core Ops, SparseCore 0:
  79.3 107.1 all-gather.1
  377.2 194.7 reduce-scatter.1
where the time goes:
time: 594 us; the launch traced here: 591 us
  waiting for transfers between devices  228 us (38%)
  local copies, waits for them, and re-layouts  198 us (33%)
  matrix products  62 us (10%)
  blocking collectives  50.6 us (9%)
  starting transfers between devices  20.7 us (3%)
  other arithmetic  16.2 us (3%)
  between operations  15 us (3%)
    reduce_scatter x1, waiting for transfers between devices, per_device(): lax.psum_scatter(attend(everyone, migrated, first, new_lengths), 'item',...  190 us
    dynamic_update_slice x16, local copies, waits for them, and re-layouts, attend(): return lax.map(one_rows, blocks).reshape(rows, sessions, width)  78.8 us
    dot_general x8, matrix products, attend_block(): jnp.einsum('shre,sehd->rshd', weights, values, preferred_element_type=jnp...  55.6 us
    unnamed x1, blocking collectives  50.6 us
    dynamic_slice x16, local copies, waits for them, and re-layouts, attend(): return lax.map(one_rows, blocks).reshape(rows, sessions, width)  32.8 us
    slice x8, local copies, waits for them, and re-layouts, attend_block(): keys = group[:, :, 0, :].reshape(sessions, span, HEADS, size)  22.6 us
    all_gather x1, waiting for transfers between devices, per_device(): everyone = lax.all_gather(queries, 'item', axis=0, tiled=True)  17.6 us
    all_to_all x1, waiting for transfers between devices, per_device(): lax.all_to_all(jnp.take(table, lax.all_to_all(requests, ('session', 'item...  13.3 us
  transfers between devices with their start and end apart: 5, of which 4 were waited for; matrix products, arithmetic and copies ran while one was open for 7% of the time, Pallas kernels for 0%

commit v1 on v0

v1 whole, which is shorter than its diff:
```python
import functools
import math

import jax
import jax.numpy as jnp
from jax import lax
from jax.experimental import pallas as pl
from jax.experimental.pallas import tpu as pltpu
from jax.sharding import PartitionSpec as P

HEADS = 4
CHUNKS = 4
ZN = 4
XN = 4
QCAP = 4
BF = jnp.bfloat16
F32 = jnp.float32
I32 = jnp.int32


def iota(shape, dim):
    return lax.broadcasted_iota(I32, shape, dim)


def dot(a, b):
    return jnp.dot(a, b, preferred_element_type=F32)


def dot_nt(a, b):
    return lax.dot_general(a, b, (((1,), (1,)), ((), ())), preferred_element_type=F32)


def kernel(
    ns_ref, ln_ref, ids_ref, inv_ref, cache_ref, table_ref, wqu_ref, wout_ref, whead_ref,
    mig_out, score_out,
    table, sendbuf, inc0, inc1, inc2, inc3, migbuf, kv,
    meta_own, meta, ns_vec, ns_smem, len_vec,
    ids_pad, inv_pad, req_own, req1, req2, req3, col, acc, resp, back, turned, fetched,
    pick, csend, cand, query, gate, mixed, ssend, sback,
    table_sem, small_sem, out_sem,
    meta_s, meta_r, m_s, m_r, z_s, z_r, x_s, x_r, f_s, f_r,
    q1_s, q1_r, q2_s, q2_r, p1_s, p1_r, p2_s, p2_r, c_s, c_r, o_s, o_r,
):
    incoming = (inc0, inc1, inc2, inc3)
    sess = lax.axis_index("session")
    item = lax.axis_index("item")
    x = item // ZN
    z = item % ZN
    span = kv.shape[4]
    width = cache_ref.shape[3]
    size = width // HEADS
    count = inv_ref.shape[1]
    items = table.shape[0]

    def speer(d):
        return lax.rem(sess + d, 8)

    def ipeer(d):
        return lax.rem(item + d, 16)

    def zpeer(d):
        return lax.rem(z + d, ZN)

    def xpeer(d):
        return lax.rem(x + d, XN)

    def remote(src, dst, ssem, rsem, s_to, i_to):
        return pltpu.make_async_remote_copy(
            src_ref=src, dst_ref=dst, send_sem=ssem, recv_sem=rsem,
            device_id=(s_to, i_to), device_id_type=pl.DeviceIdType.MESH,
        )

    def each(low, high, body):
        def step(d, carry):
            body(d)
            return carry
        lax.fori_loop(low, high, step, 0)

    load_table = pltpu.make_async_copy(table_ref, table, table_sem)
    load_table.start()

    barrier = pltpu.get_barrier_semaphore()

    def greet_session(d):
        pl.semaphore_signal(barrier, inc=1, device_id=(speer(d), item), device_id_type=pl.DeviceIdType.MESH)

    def greet_item(d):
        pl.semaphore_signal(barrier, inc=1, device_id=(sess, ipeer(d)), device_id_type=pl.DeviceIdType.MESH)

    each(1, 8, greet_session)
    each(1, 16, greet_item)

    lanes = ids_pad.shape[1]
    ids_pad[...] = jnp.full(ids_pad.shape, -1, I32)
    ids_pad[0:1, 0:ids_ref.shape[1]] = ids_ref[...]
    ids = ids_pad[0:1, :]
    holder = lax.shift_right_arithmetic(ids, 13)
    row = (ids - holder * items).astype(F32)
    peer = iota((128, lanes), 0)
    member = peer == holder
    ones = jnp.where(member, 1.0, 0.0)
    lower = jnp.where(iota((lanes, lanes), 0) <= iota((lanes, lanes), 1), 1.0, 0.0)
    rank = dot(ones.astype(BF), lower.astype(BF)) * ones
    lane = iota((128, 128), 1)
    wanted = jnp.zeros((128, 128), F32)
    for q in range(QCAP):
        one = jnp.sum(jnp.where(rank == q + 1.0, row, 0.0), axis=1, keepdims=True)
        wanted = jnp.where(lane == q, one, wanted)
    req_own[...] = wanted.astype(I32)
    place = jnp.sum(jnp.where(member, (peer * QCAP).astype(F32) + rank - 1.0, 0.0), axis=0, keepdims=True)

    meta_lane = iota((8, 128), 1)
    meta_row = iota((8, 128), 0)
    mine = jnp.zeros((8, 128), I32)
    for j in range(4):
        both = jnp.where(meta_row == 0, ns_ref[j], ln_ref[j])
        mine = jnp.where(meta_lane == j, both, mine)
    mine = jnp.where(meta_lane < 4, mine, -1)
    meta_own[...] = mine
    meta[sess] = mine

    def fill(e, d):
        to = speer(d)
        which = jnp.int32(0)
        for j in range(4):
            which = jnp.where(lax.shift_right_arithmetic(ns_ref[j], 2) == to, j, which)
        return cache_ref[which, :, e * span:(e + 1) * span, :]

    def prepare(e):
        def body(d):
            sendbuf[e, d] = fill(e, d)
        incoming[e][sess] = fill(e, 0)
        each(1, 8, body)

    def migrate(e, d):
        return remote(sendbuf.at[e, d], incoming[e].at[sess], m_s.at[e, d], m_r.at[e, d], speer(d), item)

    def request_s(d):
        to = speer(d)
        return remote(
            req_own.at[pl.ds(pl.multiple_of(to * 16, 16), 16)],
            req1.at[pl.ds(pl.multiple_of(sess * 16, 16), 16)],
            q1_s.at[d], q1_r.at[d], to, item)

    def request_i(d):
        to = ipeer(d)
        return remote(req2.at[to], req3.at[item], q2_s.at[d], q2_r.at[d], sess, to)

    def response_i(d):
        to = ipeer(d)
        return remote(resp.at[to], back.at[item], p1_s.at[d], p1_r.at[d], sess, to)

    def response_s(d):
        to = speer(d)
        return remote(turned.at[to], fetched.at[sess], p2_s.at[d], p2_r.at[d], to, item)

    def tell(d):
        return remote(meta_own, meta.at[sess], meta_s.at[d], meta_r.at[d], speer(d), item)

    def gather_z(e, d):
        to = zpeer(d)
        return remote(migbuf.at[e, to], kv.at[e, 0, ZN - d], z_s.at[e, d], z_r.at[e, d], sess, x * ZN + to)

    def ring_x(e, way):
        to = xpeer(1 if way == 0 else 3)
        return remote(kv.at[e, 0], kv.at[e, 3 if way == 0 else 1], x_s.at[e, way], x_r.at[e, way], sess, to * ZN + z)

    def forward_x(e, way):
        to = xpeer(1 if way == 0 else 3)
        part = pl.ds(0, 2) if way == 0 else pl.ds(2, 2)
        return remote(
            kv.at[e, 3 if way == 0 else 1, part], kv.at[e, 2, part],
            f_s.at[e, way], f_r.at[e, way], sess, to * ZN + z)

    def send_cand(d):
        return remote(csend.at[d], cand.at[ZN - d], c_s.at[d], c_r.at[d], sess, x * ZN + zpeer(d))

    def send_score(d):
        return remote(ssend.at[d], sback.at[ZN - d], o_s.at[d], o_r.at[d], sess, x * ZN + zpeer(d))

    prepare(0)
    pl.semaphore_wait(barrier, 22)
    each(1, 8, lambda d: request_s(d).start())
    each(1, 8, lambda d: tell(d).start())
    each(1, 8, lambda d: migrate(0, d).start())
    prepare(1)
    each(1, 8, lambda d: migrate(1, d).start())
    own = pl.ds(pl.multiple_of(sess * 16, 16), 16)
    req1[own] = req_own[own]

    each(1, 8, lambda d: request_s(d).wait_recv())
    for i in range(16):
        req2[i] = req1[pl.ds(i, 8, stride=16), :]
    req3[item] = req2[item]
    each(1, 16, lambda d: request_i(d).start())

    put = jnp.where(iota((512, lanes), 0).astype(F32) == place, 1.0, 0.0).astype(BF)
    inv_pad[...] = jnp.zeros(inv_pad.shape, F32)
    inv_pad[0:4, :] = inv_ref[...].astype(F32)
    inv_col = jnp.transpose(inv_pad[...])
    for j in range(4):
        hot = jnp.where(iota((count, lanes), 1).astype(F32) == inv_col[:, j:j + 1], 1.0, 0.0).astype(BF)
        pick[j] = dot_nt(hot, put).astype(BF)

    prepare(2)
    each(1, 8, lambda d: migrate(2, d).start())
    prepare(3)
    each(1, 8, lambda d: migrate(3, d).start())

    each(1, 8, lambda d: tell(d).wait_recv())
    slots = jnp.zeros((8, 128), I32)
    live = jnp.zeros((1, 128), I32)
    for o in range(8):
        first = meta[o, 0:1, :]
        slots = jnp.where(meta_row == o, first, slots)
        live = live + jnp.where(first == sess * 4 + z, meta[o, 1:2, :], 0)
    live = jnp.sum(live.astype(F32), axis=1, keepdims=True)
    len_vec[...] = jnp.broadcast_to(live, (8, 128)).astype(I32)
    ns_vec[...] = slots
    to_smem = pltpu.make_async_copy(ns_vec, ns_smem, small_sem)
    to_smem.start()
    to_smem.wait()

    def source(k):
        src = jnp.int32(0)
        for o in range(8):
            for j in range(4):
                src = jnp.where(ns_smem[o, j] == sess * 4 + k, o, src)
        return src

    sources = [source(k) for k in range(4)]

    def store_out(e):
        return pltpu.make_async_copy(migbuf.at[e], mig_out.at[:, :, pl.ds(e * span, span), :], out_sem.at[e])

    def settle(e):
        each(1, 8, lambda d: migrate(e, d).wait_recv())
        for k in range(4):
            migbuf[e, k] = incoming[e][sources[k]]
        kv[e, 0, 0] = migbuf[e, z]
        each(1, ZN, lambda d: gather_z(e, d).start())
        store_out(e).start()

    def spread(e):
        each(1, ZN, lambda d: gather_z(e, d).wait_recv())
        for way in range(2):
            ring_x(e, way).start()

    def onward(e):
        for way in range(2):
            ring_x(e, way).wait_recv()
            forward_x(e, way).start()

    def arrive(e):
        for way in range(2):
            forward_x(e, way).wait_recv()

    each(1, 16, lambda d: request_i(d).wait_recv())
    for i in range(16):
        asked = req3[i]
        for q in range(QCAP):
            col[i * 32 + q * 8:i * 32 + q * 8 + 8, :] = jnp.broadcast_to(asked[:, q:q + 1], (8, 128))
    load_table.wait()
    acc[...] = jnp.zeros(acc.shape, F32)
    depth = 1024

    def look_up(c):
        base = c * depth
        want = col[...] - iota(col.shape, 1) - base
        hot = jnp.concatenate(
            [jnp.where(want == t * 128, 1.0, 0.0).astype(BF) for t in range(depth // 128)], axis=1)
        acc[...] += dot(hot, table[pl.ds(pl.multiple_of(base, depth), depth), :])

    each(0, items // depth, look_up)
    for i in range(16):
        resp[i] = acc[i * 32:(i + 1) * 32, :].astype(BF)
    back[item] = resp[item]
    each(1, 16, lambda d: response_i(d).start())

    settle(0)
    settle(1)
    spread(0)

    each(1, 16, lambda d: response_i(d).wait_recv())
    out_row = iota((512, 512), 0)
    in_row = lax.rem(out_row, 64) // 4 * 32 + lax.rem(out_row, 4) * 8 + out_row // 64
    turn = jnp.where(in_row == iota((512, 512), 1), 1.0, 0.0).astype(BF)
    turned[...] = dot(turn, back[...].reshape(512, width)).astype(BF).reshape(8, 64, width)
    fetched[sess] = turned[sess]
    each(1, 8, lambda d: response_s(d).start())

    spread(1)
    onward(0)
    settle(2)
    spread(2)
    onward(1)

    each(1, 8, lambda d: response_s(d).wait_recv())

    def make_cand(d):
        return dot(pick[zpeer(d)], fetched[...].reshape(512, width)).astype(BF)

    for d in range(1, ZN):
        csend[d] = make_cand(d)
        send_cand(d).start()
    cand[0] = make_cand(0)

    settle(3)
    spread(3)
    onward(2)

    def project(r):
        rows = cand[r]
        query[r] = dot(rows, wqu_ref[:, 0:width]).astype(BF)
        g = dot(rows, wqu_ref[:, width:])
        gate[r] = g / (1.0 + jnp.exp(-g))
        mixed[r] = jnp.zeros(mixed.shape[1:], F32)

    each(1, ZN, lambda d: send_cand(d).wait_recv())
    each(0, ZN, project)

    def attend(e):
        half = 0.5 / math.sqrt(size)
        spot = iota((1, ZN * span), 1)
        where = lax.rem(z + spot // span, ZN) * (ZN * 64) + lax.rem(spot, span) + e * span
        scales = []
        for s in range(XN):
            position = xpeer(s) * (ZN * 256) + where
            alive = position < jnp.broadcast_to(len_vec[0:1, 0:1], position.shape)
            scales.append(jnp.where(alive, half, 0.0))

        def rows(r):
            for h in range(HEADS):
                cols = slice(h * size, (h + 1) * size)
                q = query[r, :, cols]
                total = mixed[r, :, cols]
                for s in range(XN):
                    keys = kv[e, s, :, 0, :, cols].reshape(ZN * span, size)
                    values = kv[e, s, :, 1, :, cols].reshape(ZN * span, size)
                    u = dot_nt(q, keys) * scales[s]
                    w = (u + u * jnp.tanh(u)).astype(BF)
                    total = total + dot(w, values)
                mixed[r, :, cols] = total

        each(0, ZN, rows)

    arrive(0)
    attend(0)
    onward(3)
    arrive(1)
    attend(1)
    arrive(2)
    attend(2)
    arrive(3)
    attend(3)

    head = jnp.broadcast_to(whead_ref[...], (16, width))
    fold = dot_nt(head, wout_ref[...])
    fold0 = fold.astype(BF)
    left = fold - fold0.astype(F32)
    fold1 = left.astype(BF)
    fold2 = (left - fold1.astype(F32)).astype(BF)
    which_row = iota((16, width), 0)
    folds = jnp.where(
        which_row == 0, fold0.astype(F32),
        jnp.where(which_row == 1, fold1.astype(F32), jnp.where(which_row == 2, fold2.astype(F32), 0.0))).astype(BF)
    heads = jnp.where(which_row == 0, head.astype(F32), 0.0).astype(BF)

    def finish(r):
        m = mixed[r]
        normed = m * lax.rsqrt(jnp.mean(m * m, axis=1, keepdims=True) + 1e-6)
        gated = (normed * gate[r]).astype(BF)
        part = dot_nt(folds, gated) + dot_nt(heads, cand[r])
        line = jnp.sum(part, axis=0, keepdims=True)
        ssend[r] = jnp.broadcast_to(line, (8, count))

    def finish_send(d):
        finish(d)
        send_score(d).start()

    each(1, ZN, finish_send)
    finish(0)
    sback[0] = ssend[0]
    each(1, ZN, lambda d: send_score(d).wait_recv())
    for j in range(4):
        score_out[j:j + 1, :] = sback[lax.rem(j - z + ZN, ZN), 0:1, :]

    each(1, 8, lambda d: request_s(d).wait_send())
    each(1, 8, lambda d: tell(d).wait_send())
    each(1, 16, lambda d: request_i(d).wait_send())
    each(1, 16, lambda d: response_i(d).wait_send())
    each(1, 8, lambda d: response_s(d).wait_send())
    each(1, ZN, lambda d: send_cand(d).wait_send())
    each(1, ZN, lambda d: send_score(d).wait_send())
    for e in range(CHUNKS):
        each(1, 8, lambda d: migrate(e, d).wait_send())
        each(1, ZN, lambda d: gather_z(e, d).wait_send())
        for way in range(2):
            ring_x(e, way).wait_send()
            forward_x(e, way).wait_send()
        store_out(e).wait()


def per_device(cache, lengths, new_slot, unique_ids, inverse, table, w_qu, w_out, w_head):
    sessions, events, _, width = cache.shape
    span = events // CHUNKS
    count = inverse.shape[1]
    split = cache.transpose(0, 2, 1, 3)
    vm = pl.BlockSpec(memory_space=pltpu.VMEM)
    sm = pl.BlockSpec(memory_space=pltpu.SMEM)
    hb = pl.BlockSpec(memory_space=pl.ANY)
    dma = pltpu.SemaphoreType.DMA
    chunk = (2, span, width)
    scratch = [
        pltpu.VMEM(table.shape, BF),
        pltpu.VMEM((CHUNKS, 8) + chunk, BF),
        pltpu.VMEM((8,) + chunk, BF),
        pltpu.VMEM((8,) + chunk, BF),
        pltpu.VMEM((8,) + chunk, BF),
        pltpu.VMEM((8,) + chunk, BF),
        pltpu.VMEM((CHUNKS, 4) + chunk, BF),
        pltpu.VMEM((CHUNKS, XN, ZN) + chunk, BF),
        pltpu.VMEM((8, 128), I32),
        pltpu.VMEM((8, 8, 128), I32),
        pltpu.VMEM((8, 128), I32),
        pltpu.SMEM((8, 128), I32),
        pltpu.VMEM((8, 128), I32),
        pltpu.VMEM((8, 384), I32),
        pltpu.VMEM((8, count), F32),
        pltpu.VMEM((128, 128), I32),
        pltpu.VMEM((128, 128), I32),
        pltpu.VMEM((16, 8, 128), I32),
        pltpu.VMEM((16, 8, 128), I32),
        pltpu.VMEM((512, 128), I32),
        pltpu.VMEM((512, width), F32),
        pltpu.VMEM((16, 32, width), BF),
        pltpu.VMEM((16, 32, width), BF),
        pltpu.VMEM((8, 64, width), BF),
        pltpu.VMEM((8, 64, width), BF),
        pltpu.VMEM((4, count, 512), BF),
        pltpu.VMEM((4, count, width), BF),
        pltpu.VMEM((4, count, width), BF),
        pltpu.VMEM((4, count, width), BF),
        pltpu.VMEM((4, count, width), F32),
        pltpu.VMEM((4, count, width), F32),
        pltpu.VMEM((4, 8, count), F32),
        pltpu.VMEM((4, 8, count), F32),
        dma, dma, dma((CHUNKS,)),
        dma((8,)), dma((8,)),
        dma((CHUNKS, 8)), dma((CHUNKS, 8)),
        dma((CHUNKS, ZN)), dma((CHUNKS, ZN)),
        dma((CHUNKS, 2)), dma((CHUNKS, 2)),
        dma((CHUNKS, 2)), dma((CHUNKS, 2)),
        dma((8,)), dma((8,)), dma((16,)), dma((16,)),
        dma((16,)), dma((16,)), dma((8,)), dma((8,)),
        dma((ZN,)), dma((ZN,)), dma((ZN,)), dma((ZN,)),
    ]
    migrated, scores = pl.pallas_call(
        kernel,
        out_shape=(
            jax.ShapeDtypeStruct(split.shape, BF),
            jax.ShapeDtypeStruct((sessions, count), F32),
        ),
        in_specs=[sm, sm, vm, vm, vm, hb, vm, vm, vm],
        out_specs=(hb, vm),
        scratch_shapes=scratch,
        compiler_params=pltpu.CompilerParams(
            collective_id=0, has_side_effects=True, vmem_limit_bytes=56 * 1024 * 1024),
        cost_estimate=pl.CostEstimate(flops=12_000_000_000, bytes_accessed=16_000_000, transcendentals=17_000_000),
    )(new_slot, lengths, unique_ids, inverse, split, table, w_qu, w_out, w_head.reshape(1, width))
    return migrated.transpose(0, 2, 1, 3), scores


def solution(mesh):
    placed = (
        P("session", "item", None, None),
        P("session"),
        P("session"),
        P("session", "item"),
        P("session", "item"),
        P(("session", "item"), None),
        P(),
        P(),
        P(),
    )
    return jax.shard_map(
        per_device,
        mesh=mesh,
        in_specs=placed,
        out_specs=(P("session", "item", None, None), P("session", "item")),
        check_vma=False,
    )
```

time: 594 us -> 135 us (0.23)
  waiting for transfers between devices: 228 us -> 0 us
  local copies, waits for them, and re-layouts: 198 us -> 10.2 us
  Pallas kernels: 0 us -> 124 us
  matrix products: 62 us -> 0 us
  blocking collectives: 50.6 us -> 0 us
  starting transfers between devices: 20.7 us -> 0 us
  other arithmetic: 16.2 us -> 0 us
  between operations: 15 us -> 0.65 us
    reduce_scatter x1 -> x0, waiting for transfers between devices: 190 us -> none  [per_device(): lax.psum_scatter(attend(everyone, migrated, first, new_lengths), 'item',...]
    pallas_call x0 -> x1, Pallas kernels: none -> 124 us  [per_device(): pl.pallas_call(kernel, out_shape=(jax.ShapeDtypeStruct(split.shape, BF),...]
    dynamic_update_slice x16 -> x0, local copies, waits for them, and re-layouts: 78.8 us -> none  [attend(): return lax.map(one_rows, blocks).reshape(rows, sessions, width)]
    dot_general x10 -> x0, matrix products: 62 us -> none  [the longest x8 55.6 us: attend_block(): jnp.einsum('shre,sehd->rshd', weights, values, preferred_element_type=jnp...]
    unnamed x1 -> x0, blocking collectives: 50.6 us -> none
    dynamic_slice x16 -> x0, local copies, waits for them, and re-layouts: 32.8 us -> none  [attend(): return lax.map(one_rows, blocks).reshape(rows, sessions, width)]
    gather x7 -> x0, local copies, waits for them, and re-layouts: 29.3 us -> none  [the longest x1 9.76 us: per_device(): jnp.take(cache, which, axis=0)]
    slice x9 -> x0, local copies, waits for them, and re-layouts: 23.8 us -> none  [the longest x8 22.6 us: attend_block(): keys = group[:, :, 0, :].reshape(sessions, span, HEADS, size)]
  transfers between devices with their start and end apart: 5 -> 0, of which waited for: 4 -> 0; matrix products, arithmetic and copies ran while one was open for 7% -> 0% of each run, Pallas kernels for 0% -> 0%
where the time goes in v1:
time: 135 us
  Pallas kernels  124 us (92%)
  local copies, waits for them, and re-layouts  10.2 us (8%)
    pallas_call x1, Pallas kernels, per_device(): pl.pallas_call(kernel, out_shape=(jax.ShapeDtypeStruct(split.shape, BF),...  124 us
    unnamed x5, local copies, waits for them, and re-layouts  8.94 us

profile of v1, /device:TPU:0, one launch (start us, length us, event | category | flops | bytes accessed | tf_op | source)
XLA Modules:
  0.0 135.0 jit_solution(2889518186255400100)
XLA Ops:
  0.6 1.3 reshape.7.whead_ref
  1.9 3.3 %copy.14 = bf16[4,256,2,512]{3,1,2,0:T(8,128)(2,1)} copy(bf16[4,256,2,512]{3,2,1,0:T(2,128)(2,1)} %param.9) | data formatting | bytes 4194304 | tf_op args[0]
  5.2 124.1 %shard_map.104 = (bf16[4,2,256,512]{3,2,1,0:T(8,128)(2,1)}, f32[4,256]{1,0:T(4,128)}) custom-call(s32[4]{0:T(128)} %ns_ref.1, s32[4]{0:T(128)} %ln_ref.1, s32[1,320]{1,0:T(1,128)} %ids_ref.1, s32[4,256]{1,0:T(4,128)} %inv_ref.1, bf16[4,2,256,512]{3,2,1,0:T(8,128)(2,1)} %bitcast.5, bf16[8192,512]{1,0:T(8,128)(2,1)} %table_ref.1, bf16[512,1024]{1,0:T(8,128)(2,1)} %wqu_ref.1, ...), custom_call_target="tpu_custom_call" | custom-call | flops 12000000000 | bytes 16000000 | tf_op jit(solution)/shard_map/pallas_call | solution.py:458
  129.3 0.0 copy-start
  129.3 5.1 %copy.12 = bf16[4,256,2,512]{3,2,1,0:T(2,128)(2,1)} copy(bf16[4,256,2,512]{3,1,2,0:T(8,128)(2,1)} %bitcast.4) | data formatting | bytes 4194304
  134.4 0.0 copy-done
  134.4 0.6 copy.16
Async XLA Ops:
  129.3 5.1 %copy-start = (f32[4,256]{1,0:T(4,128)S(1)}, f32[4,256]{1,0:T(4,128)}, u32[]{:S(2)}) copy-start(f32[4,256]{1,0:T(4,128)} %get-tuple-element.11) | copy-start | bytes 12292

commit v2 on v1

v2 whole, which is shorter than its diff:
```python
import functools
import math

import jax
import jax.numpy as jnp
from jax import lax
from jax.experimental import pallas as pl
from jax.experimental.pallas import tpu as pltpu
from jax.sharding import PartitionSpec as P

HEADS = 4
CHUNKS = 8
AHEAD = 2
ZN = 4
XN = 4
QCAP = 4
BF = jnp.bfloat16
F32 = jnp.float32
I32 = jnp.int32


def iota(shape, dim):
    return lax.broadcasted_iota(I32, shape, dim)


def dot(a, b):
    return jnp.dot(a, b, preferred_element_type=F32)


def dot_nt(a, b):
    return lax.dot_general(a, b, (((1,), (1,)), ((), ())), preferred_element_type=F32)


def kernel(
    ns_ref, ln_ref, ids_ref, inv_ref, cache_hbm, table_ref, wqu_hbm, wout_hbm, whead_ref,
    mig_out, score_out,
    cache_ref, wqu_ref, wout_ref, table, sendbuf, inc0, inc1, inc2, inc3, inc4, inc5, inc6, inc7, migbuf, split, parted, kv,
    meta_own, meta, ns_vec, ns_smem, len_vec,
    ids_pad, inv_pad, req_own, req1, req2, req3, col, acc, resp, back, turned, fetched,
    turn, pick, csend, cand, query, gate, mixed, ssend, sback,
    cache_sem, wqu_sem, wout_sem, table_sem, small_sem, out_sem,
    meta_s, meta_r, m_s, m_r, z_s, z_r, x_s, x_r, f_s, f_r,
    q1_s, q1_r, q2_s, q2_r, p1_s, p1_r, p2_s, p2_r, c_s, c_r, o_s, o_r,
):
    incoming = (inc0, inc1, inc2, inc3, inc4, inc5, inc6, inc7)
    sess = lax.axis_index("session")
    item = lax.axis_index("item")
    x = item // ZN
    z = item % ZN
    span = kv.shape[4]
    block = 2 * HEADS * span
    width = wout_ref.shape[0]
    size = width // HEADS
    count = inv_ref.shape[1]
    items = table.shape[0]

    def speer(d):
        return lax.rem(sess + d, 8)

    def ipeer(d):
        return lax.rem(item + d, 16)

    core = lax.rem(sess, 2)
    sx = lax.rem(x + XN - core, XN)
    sz = lax.rem(z + ZN - core, ZN)
    px = sx + 1 - 2 * lax.rem(sx, 2)
    pz = sz + 1 - 2 * lax.rem(sz, 2)

    def device(ax, az):
        return lax.rem(ax + core, XN) * ZN + lax.rem(az + core, ZN)

    def mirror(g):
        return sx + g // 2 * (3 - 2 * sx), sz + g % 2 * (3 - 2 * sz)

    def square(ax, az):
        return ax // 2 * 2 + az // 2

    def session_of(g):
        return square(*mirror(g))

    def remote(src, dst, ssem, rsem, s_to, i_to):
        return pltpu.make_async_remote_copy(
            src_ref=src, dst_ref=dst, send_sem=ssem, recv_sem=rsem,
            device_id=(s_to, i_to), device_id_type=pl.DeviceIdType.MESH,
        )

    def each(low, high, body):
        def step(d, carry):
            body(d)
            return carry
        lax.fori_loop(low, high, step, 0)

    def wait_bytes(ref, sem):
        pltpu.make_async_copy(ref, ref, sem).wait()

    load_cache = pltpu.make_async_copy(cache_hbm, cache_ref, cache_sem)
    load_cache.start()
    load_table = pltpu.make_async_copy(table_ref, table, table_sem)
    load_table.start()
    load_wqu = pltpu.make_async_copy(wqu_hbm, wqu_ref, wqu_sem)
    load_wqu.start()
    load_wout = pltpu.make_async_copy(wout_hbm, wout_ref, wout_sem)
    load_wout.start()

    barrier = pltpu.get_barrier_semaphore()

    def greet_session(d):
        pl.semaphore_signal(barrier, inc=1, device_id=(speer(d), item), device_id_type=pl.DeviceIdType.MESH)

    def greet_item(d):
        pl.semaphore_signal(barrier, inc=1, device_id=(sess, ipeer(d)), device_id_type=pl.DeviceIdType.MESH)

    each(1, 8, greet_session)
    each(1, 16, greet_item)

    lanes = ids_pad.shape[1]
    ids_pad[...] = jnp.full(ids_pad.shape, -1, I32)
    ids_pad[0:1, 0:ids_ref.shape[1]] = ids_ref[...]
    ids = ids_pad[0:1, :]
    holder = lax.shift_right_arithmetic(ids, 13)
    row = (ids - holder * items).astype(F32)
    peer = iota((128, lanes), 0)
    member = peer == holder
    ones = jnp.where(member, 1.0, 0.0)
    lower = jnp.where(iota((lanes, lanes), 0) <= iota((lanes, lanes), 1), 1.0, 0.0)
    rank = dot(ones.astype(BF), lower.astype(BF)) * ones
    lane = iota((128, 128), 1)
    wanted = jnp.zeros((128, 128), F32)
    for q in range(QCAP):
        one = jnp.sum(jnp.where(rank == q + 1.0, row, 0.0), axis=1, keepdims=True)
        wanted = jnp.where(lane == q, one, wanted)
    req_own[...] = wanted.astype(I32)
    place = jnp.sum(jnp.where(member, (peer * QCAP).astype(F32) + rank - 1.0, 0.0), axis=0, keepdims=True)

    meta_lane = iota((8, 128), 1)
    meta_row = iota((8, 128), 0)
    mine = jnp.zeros((8, 128), I32)
    for j in range(4):
        both = jnp.where(meta_row == 0, ns_ref[j], ln_ref[j])
        mine = jnp.where(meta_lane == j, both, mine)
    mine = jnp.where(meta_lane < 4, mine, -1)
    meta_own[...] = mine
    meta[sess] = mine

    def fill(e, d):
        to = speer(d)
        which = jnp.int32(0)
        for j in range(4):
            which = jnp.where(lax.shift_right_arithmetic(ns_ref[j], 2) == to, j, which)
        return cache_ref[which, e * block:(e + 1) * block, :]

    def prepare(e):
        def body(d):
            sendbuf[e, d] = fill(e, d)
        incoming[e][sess] = fill(e, 0)
        each(1, 8, body)

    def migrate(e, d):
        return remote(sendbuf.at[e, d], incoming[e].at[sess], m_s, m_r.at[e], speer(d), item)

    def request_s(d):
        to = speer(d)
        return remote(
            req_own.at[pl.ds(pl.multiple_of(to * 16, 16), 16)],
            req1.at[pl.ds(pl.multiple_of(sess * 16, 16), 16)],
            q1_s, q1_r, to, item)

    def request_i(d):
        to = ipeer(d)
        return remote(req2.at[to], req3.at[item], q2_s, q2_r, sess, to)

    def response_i(d):
        to = ipeer(d)
        return remote(resp.at[to], back.at[item], p1_s, p1_r, sess, to)

    def response_s(d):
        to = speer(d)
        return remote(turned.at[to], fetched.at[sess], p2_s, p2_r, to, item)

    def tell(d):
        return remote(meta_own, meta.at[sess], meta_s, meta_r, speer(d), item)

    def enter(e, g):
        return remote(
            parted.at[e, session_of(g)], kv.at[e, 0, g], z_s, z_r.at[e], sess, device(*mirror(g)))

    def pair(e, way):
        to = device(px, sz) if way == 0 else device(sx, pz)
        return remote(kv.at[e, 0], kv.at[e, 2 if way == 0 else 1], x_s, x_r.at[e], sess, to)

    def across(e, way):
        to = device(sx, pz) if way == 0 else device(px, sz)
        part = pl.ds(0, 2) if way == 0 else pl.ds(2, 2)
        return remote(
            kv.at[e, 2 if way == 0 else 1, part], kv.at[e, 3, part], f_s, f_r.at[e], sess, to)

    def send_cand(g):
        return remote(csend.at[g], cand.at[g], c_s, c_r, sess, device(*mirror(g)))

    def send_score(g):
        return remote(ssend.at[g], sback.at[g], o_s, o_r, sess, device(*mirror(g)))

    def settle(e):
        wait_bytes(incoming[e].at[pl.ds(0, 7)], m_r.at[e])
        if e + AHEAD < CHUNKS:
            prepare(e + AHEAD)
            each(1, 8, lambda d: migrate(e + AHEAD, d).start())
        for k in range(4):
            rows = incoming[e][sources[k]]
            migbuf[e, k] = rows
            parted[e, k] = dot(split[...], rows).astype(BF).reshape(2 * HEADS, span, size)
        each(1, 4, lambda g: enter(e, g).start())
        kv[e, 0, 0] = parted[e, session_of(0)]
        store_out(e).start()

    def spread(e):
        wait_bytes(kv.at[e, 0, pl.ds(0, 3)], z_r.at[e])
        for way in range(2):
            pair(e, way).start()

    def onward(e):
        wait_bytes(kv.at[e, pl.ds(1, 2)], x_r.at[e])
        for way in range(2):
            across(e, way).start()

    def arrive(e):
        wait_bytes(kv.at[e, 3], f_r.at[e])

    def store_out(e):
        return pltpu.make_async_copy(migbuf.at[e], mig_out.at[:, pl.ds(e * block, block), :], out_sem)

    load_cache.wait()
    for e in range(AHEAD):
        prepare(e)
    pl.semaphore_wait(barrier, 22)
    each(1, 8, lambda d: request_s(d).start())
    each(1, 8, lambda d: tell(d).start())
    for e in range(AHEAD):
        each(1, 8, functools.partial(lambda e, d: migrate(e, d).start(), e))
    own = pl.ds(pl.multiple_of(sess * 16, 16), 16)
    req1[own] = req_own[own]

    to_row = iota((block, block), 0)
    from_row = lax.rem(to_row, span) * (2 * HEADS) + to_row // span
    split[...] = jnp.where(from_row == iota((block, block), 1), 1.0, 0.0).astype(BF)
    put = jnp.where(iota((512, lanes), 0).astype(F32) == place, 1.0, 0.0).astype(BF)
    inv_pad[...] = jnp.zeros(inv_pad.shape, F32)
    inv_pad[0:4, :] = inv_ref[...].astype(F32)
    inv_col = jnp.transpose(inv_pad[...])
    for j in range(4):
        hot = jnp.where(iota((count, lanes), 1).astype(F32) == inv_col[:, j:j + 1], 1.0, 0.0).astype(BF)
        pick[j] = dot_nt(hot, put).astype(BF)
    out_row = iota((512, 512), 0)
    in_row = lax.rem(out_row, 64) // 4 * 32 + lax.rem(out_row, 4) * 8 + out_row // 64
    turn[...] = jnp.where(in_row == iota((512, 512), 1), 1.0, 0.0).astype(BF)

    wait_bytes(req1.at[pl.ds(0, 112)], q1_r)
    for i in range(16):
        req2[i] = req1[pl.ds(i, 8, stride=16), :]
    req3[item] = req2[item]
    each(1, 16, lambda d: request_i(d).start())

    wait_bytes(meta.at[pl.ds(0, 7)], meta_r)
    slots = jnp.zeros((8, 128), I32)
    live = jnp.zeros((1, 128), I32)
    for o in range(8):
        first = meta[o, 0:1, :]
        slots = jnp.where(meta_row == o, first, slots)
        live = live + jnp.where(first == sess * 4 + session_of(0), meta[o, 1:2, :], 0)
    live = jnp.sum(live.astype(F32), axis=1, keepdims=True)
    len_vec[...] = jnp.broadcast_to(live, (8, 128)).astype(I32)
    ns_vec[...] = slots
    to_smem = pltpu.make_async_copy(ns_vec, ns_smem, small_sem)
    to_smem.start()
    to_smem.wait()

    def source(k):
        src = jnp.int32(0)
        for o in range(8):
            for j in range(4):
                src = jnp.where(ns_smem[o, j] == sess * 4 + k, o, src)
        return src

    sources = [source(k) for k in range(4)]

    settle(0)
    settle(1)

    wait_bytes(req3.at[pl.ds(0, 15)], q2_r)
    for i in range(16):
        asked = req3[i]
        for q in range(QCAP):
            col[i * 32 + q * 8:i * 32 + q * 8 + 8, :] = jnp.broadcast_to(asked[:, q:q + 1], (8, 128))
    load_table.wait()
    acc[...] = jnp.zeros(acc.shape, F32)
    depth = 1024

    def look_up(c):
        base = c * depth
        want = col[...] - iota(col.shape, 1) - base
        hot = jnp.concatenate(
            [jnp.where(want == t * 128, 1.0, 0.0).astype(BF) for t in range(depth // 128)], axis=1)
        acc[...] += dot(hot, table[pl.ds(pl.multiple_of(base, depth), depth), :])

    def look_ups(c):
        @pl.when(c == items // depth // 2)
        def _():
            spread(0)
            spread(1)

        look_up(c)

    each(0, items // depth, look_ups)
    for i in range(16):
        resp[i] = acc[i * 32:(i + 1) * 32, :].astype(BF)
    back[item] = resp[item]
    each(1, 16, lambda d: response_i(d).start())

    settle(2)
    onward(0)
    settle(3)
    onward(1)
    spread(2)

    wait_bytes(back.at[pl.ds(0, 15)], p1_r)
    turned[...] = dot(turn[...], back[...].reshape(512, width)).astype(BF).reshape(8, 64, width)
    fetched[sess] = turned[sess]
    each(1, 8, lambda d: response_s(d).start())

    settle(4)
    spread(3)
    onward(2)
    settle(5)
    spread(4)
    onward(3)

    wait_bytes(fetched.at[pl.ds(0, 7)], p2_r)

    def make_cand(g):
        return dot(pick[session_of(g)], fetched[...].reshape(512, width)).astype(BF)

    for g in range(1, 4):
        csend[g] = make_cand(g)
        send_cand(g).start()
    cand[0] = make_cand(0)

    settle(6)
    spread(5)
    onward(4)
    settle(7)
    spread(6)
    onward(5)

    load_wqu.wait()

    def project(r):
        rows = cand[r]
        query[r] = dot(rows, wqu_ref[:, 0:width]).astype(BF)
        g = dot(rows, wqu_ref[:, width:])
        gate[r] = g / (1.0 + jnp.exp(-g))
        mixed[r] = jnp.zeros(mixed.shape[1:], F32)

    wait_bytes(cand.at[pl.ds(1, 3)], c_r)
    each(0, 4, project)

    def attend(p):
        e = 2 * p

        @pl.when(p == 1)
        def _():
            spread(7)
            onward(6)

        @pl.when(p == 2)
        def _():
            onward(7)

        arrive(e)
        arrive(e + 1)
        half = 0.5 / math.sqrt(size)
        spot = iota((1, 8 * span), 1)
        group = lax.rem(spot, 4 * span) // span
        event = (e + spot // (4 * span)) * span + lax.rem(spot, span)
        scales = []
        for m in range(4):
            ax, az = (px if m // 2 else sx), (pz if m % 2 else sz)
            gx = ax + group // 2 * (3 - 2 * ax)
            gz = az + lax.rem(group, 2) * (3 - 2 * az)
            position = device(gx, gz) * (CHUNKS * span) + event
            alive = position < jnp.broadcast_to(len_vec[0:1, 0:1], position.shape)
            scales.append(jnp.where(alive, half, 0.0))

        def rows(r):
            for h in range(HEADS):
                cols = slice(h * size, (h + 1) * size)
                q = query[r, :, cols]
                total = mixed[r, :, cols]
                for m in range(4):
                    keys = kv[pl.ds(e, 2), m, :, 2 * h].reshape(8 * span, size)
                    values = kv[pl.ds(e, 2), m, :, 2 * h + 1].reshape(8 * span, size)
                    u = dot_nt(q, keys) * scales[m]
                    w = (u + u * jnp.tanh(u)).astype(BF)
                    total = total + dot(w, values)
                mixed[r, :, cols] = total

        each(0, 4, rows)

    each(0, CHUNKS // 2, attend)

    load_wout.wait()
    head = jnp.broadcast_to(whead_ref[...].astype(F32).reshape(1, width), (16, width)).astype(BF)
    fold = dot_nt(head, wout_ref[...])
    fold0 = fold.astype(BF)
    left = fold - fold0.astype(F32)
    fold1 = left.astype(BF)
    fold2 = (left - fold1.astype(F32)).astype(BF)
    which_row = iota((16, width), 0)
    folds = jnp.where(
        which_row == 0, fold0.astype(F32),
        jnp.where(which_row == 1, fold1.astype(F32), jnp.where(which_row == 2, fold2.astype(F32), 0.0))).astype(BF)
    heads = jnp.where(which_row == 0, head.astype(F32), 0.0).astype(BF)

    def finish(r):
        m = mixed[r]
        normed = m * lax.rsqrt(jnp.mean(m * m, axis=1, keepdims=True) + 1e-6)
        gated = (normed * gate[r]).astype(BF)
        part = dot_nt(folds, gated) + dot_nt(heads, cand[r])
        line = jnp.sum(part, axis=0, keepdims=True)
        ssend[r] = jnp.broadcast_to(line, (8, count))

    def finish_send(g):
        finish(g)
        send_score(g).start()

    each(1, 4, finish_send)
    finish(0)
    sback[0] = ssend[0]

    wait_bytes(req_own.at[pl.ds(0, 112)], q1_s)
    wait_bytes(meta.at[pl.ds(0, 7)], meta_s)
    wait_bytes(req2.at[pl.ds(0, 15)], q2_s)
    wait_bytes(resp.at[pl.ds(0, 15)], p1_s)
    wait_bytes(turned.at[pl.ds(0, 7)], p2_s)
    wait_bytes(csend.at[pl.ds(1, 3)], c_s)
    wait_bytes(sendbuf.at[:, pl.ds(1, 7)], m_s)
    wait_bytes(parted.at[:, pl.ds(0, 3)], z_s)
    wait_bytes(kv.at[:, pl.ds(1, 2)], x_s)
    wait_bytes(kv.at[:, 3], f_s)
    wait_bytes(migbuf, out_sem)
    wait_bytes(ssend.at[pl.ds(1, 3)], o_s)

    wait_bytes(sback.at[pl.ds(1, 3)], o_r)
    for j in range(4):
        line = jnp.zeros((1, count), F32)
        for g in range(4):
            line = jnp.where(session_of(g) == j, sback[g, 0:1, :], line)
        score_out[j:j + 1, :] = line


def hand_on(mig_ref, score_ref, mig_out, score_out, held, in_sem, out_sem):
    parts = 4
    span = mig_ref.shape[1] // parts
    pieces = [(k, pl.ds(t * span, span)) for k in range(mig_ref.shape[0]) for t in range(parts)]
    loads = [
        pltpu.make_async_copy(mig_ref.at[k, part], held.at[k, part], in_sem.at[n])
        for n, (k, part) in enumerate(pieces)]
    stores = [
        pltpu.make_async_copy(held.at[k, part], mig_out.at[k, part], out_sem.at[n])
        for n, (k, part) in enumerate(pieces)]
    for load in loads:
        load.start()
    score_out[...] = score_ref[...]
    for load, store in zip(loads, stores):
        load.wait()
        store.start()
    for store in stores:
        store.wait()


def per_device(cache, lengths, new_slot, unique_ids, inverse, table, w_qu, w_out, w_head):
    sessions, events, _, width = cache.shape
    span = events // CHUNKS
    count = inverse.shape[1]
    size = width // HEADS
    block = 2 * HEADS * span
    whole = cache.reshape(sessions, events, 2, HEADS, size).transpose(0, 1, 3, 2, 4)
    whole = whole.reshape(sessions, events * HEADS * 2, size)
    vm = pl.BlockSpec(memory_space=pltpu.VMEM)
    sm = pl.BlockSpec(memory_space=pltpu.SMEM)
    hb = pl.BlockSpec(memory_space=pl.ANY)
    dma = pltpu.SemaphoreType.DMA
    chunk = (block, size)
    scratch = [
        pltpu.VMEM(whole.shape, BF),
        pltpu.VMEM(w_qu.shape, BF),
        pltpu.VMEM(w_out.shape, BF),
        pltpu.VMEM(table.shape, BF),
        pltpu.VMEM((CHUNKS, 8) + chunk, BF),
        *[pltpu.VMEM((8,) + chunk, BF) for _ in range(CHUNKS)],
        pltpu.VMEM((CHUNKS, 4) + chunk, BF),
        pltpu.VMEM((block, block), BF),
        pltpu.VMEM((CHUNKS, 4, 2 * HEADS, span, size), BF),
        pltpu.VMEM((CHUNKS, 4, 4, 2 * HEADS, span, size), BF),
        pltpu.VMEM((8, 128), I32),
        pltpu.VMEM((8, 8, 128), I32),
        pltpu.VMEM((8, 128), I32),
        pltpu.SMEM((8, 128), I32),
        pltpu.VMEM((8, 128), I32),
        pltpu.VMEM((8, 384), I32),
        pltpu.VMEM((8, count), F32),
        pltpu.VMEM((128, 128), I32),
        pltpu.VMEM((128, 128), I32),
        pltpu.VMEM((16, 8, 128), I32),
        pltpu.VMEM((16, 8, 128), I32),
        pltpu.VMEM((512, 128), I32),
        pltpu.VMEM((512, width), F32),
        pltpu.VMEM((16, 32, width), BF),
        pltpu.VMEM((16, 32, width), BF),
        pltpu.VMEM((8, 64, width), BF),
        pltpu.VMEM((8, 64, width), BF),
        pltpu.VMEM((512, 512), BF),
        pltpu.VMEM((4, count, 512), BF),
        pltpu.VMEM((4, count, width), BF),
        pltpu.VMEM((4, count, width), BF),
        pltpu.VMEM((4, count, width), BF),
        pltpu.VMEM((4, count, width), F32),
        pltpu.VMEM((4, count, width), F32),
        pltpu.VMEM((4, 8, count), F32),
        pltpu.VMEM((4, 8, count), F32),
        dma, dma, dma, dma, dma, dma,
        dma, dma,
        dma, dma((CHUNKS,)),
        dma, dma((CHUNKS,)),
        dma, dma((CHUNKS,)),
        dma, dma((CHUNKS,)),
        dma, dma, dma, dma,
        dma, dma, dma, dma,
        dma, dma, dma, dma,
    ]
    migrated, scores = pl.pallas_call(
        kernel,
        out_shape=(
            jax.ShapeDtypeStruct(whole.shape, BF),
            jax.ShapeDtypeStruct((sessions, count), F32),
        ),
        in_specs=[sm, sm, vm, vm, hb, hb, hb, hb, vm],
        out_specs=(hb, vm),
        scratch_shapes=scratch,
        compiler_params=pltpu.CompilerParams(
            collective_id=0, has_side_effects=True, vmem_limit_bytes=56 * 1024 * 1024),
        cost_estimate=pl.CostEstimate(flops=12_000_000_000, bytes_accessed=16_000_000, transcendentals=17_000_000),
    )(new_slot, lengths, unique_ids, inverse, whole, table, w_qu, w_out, w_head)
    migrated, scores = pl.pallas_call(
        hand_on,
        out_shape=(
            jax.ShapeDtypeStruct(whole.shape, BF),
            jax.ShapeDtypeStruct((sessions, count), F32),
        ),
        in_specs=[hb, vm],
        out_specs=(hb, vm),
        scratch_shapes=[pltpu.VMEM(whole.shape, BF), dma((16,)), dma((16,))],
    )(migrated, scores)
    migrated = migrated.reshape(sessions, events, HEADS, 2, size).transpose(0, 1, 3, 2, 4)
    return migrated.reshape(cache.shape), scores


def solution(mesh):
    placed = (
        P("session", "item", None, None),
        P("session"),
        P("session"),
        P("session", "item"),
        P("session", "item"),
        P(("session", "item"), None),
        P(),
        P(),
        P(),
    )
    return jax.shard_map(
        per_device,
        mesh=mesh,
        in_specs=placed,
        out_specs=(P("session", "item", None, None), P("session", "item")),
        check_vma=False,
    )
```

time: 135 us -> 110 us (0.81)
  Pallas kernels: 124 us -> 110 us
  local copies, waits for them, and re-layouts: 10.2 us -> 0 us
    pallas_call x1 -> x2, Pallas kernels: 124 us -> 110 us  [the longest x1 106 us: per_device(): pl.pallas_call(kernel, out_shape=(jax.ShapeDtypeStruct(whole.shape, BF),...]
    unnamed x5 -> x0, local copies, waits for them, and re-layouts: 8.94 us -> none
where the time goes in v2:
time: 110 us
  Pallas kernels  110 us (100%)
    pallas_call x1, Pallas kernels, per_device(): pl.pallas_call(kernel, out_shape=(jax.ShapeDtypeStruct(whole.shape, BF),...  106 us
    pallas_call x1, Pallas kernels, per_device(): pl.pallas_call(hand_on, out_shape=(jax.ShapeDtypeStruct(whole.shape, BF),...  3.84 us

profile of v2, /device:TPU:0, one launch (start us, length us, event | category | flops | bytes accessed | tf_op | source)
XLA Modules:
  0.0 110.1 jit_solution(17135702173578664892)
XLA Ops:
  0.6 105.7 %shard_map.104 = (bf16[4,2048,128]{2,1,0:T(8,128)(2,1)}, f32[4,256]{1,0:T(4,128)}) custom-call(s32[4]{0:T(128)} %ns_ref.1, s32[4]{0:T(128)} %ln_ref.1, s32[1,320]{1,0:T(1,128)} %ids_ref.1, s32[4,256]{1,0:T(4,128)} %inv_ref.1, bf16[4,2048,128]{2,1,0:T(8,128)(2,1)} %bitcast.10, bf16[8192,512]{1,0:T(8,128)(2,1)} %table_ref.1, bf16[512,1024]{1,0:T(8,128)(2,1)} %wqu_hbm.1, ...), custom_call_target="tpu_custom_call" | custom-call | flops 12000000000 | bytes 16000000 | tf_op jit(solution)/shard_map/pallas_call | solution.py:540
  106.3 3.8 %shard_map.105 = (bf16[4,2048,128]{2,1,0:T(8,128)(2,1)}, f32[4,256]{1,0:T(4,128)}) custom-call(bf16[4,2048,128]{2,1,0:T(8,128)(2,1)} %get-tuple-element.6.mig_ref, f32[4,256]{1,0:T(4,128)} %get-tuple-element.7.score_ref), custom_call_target="tpu_custom_call" | custom-call | tf_op jit(solution)/shard_map/pallas_call | solution.py:553

commit v3 on v2

--- a/solution.py
+++ b/solution.py
@@ -14,6 +14,12 @@
 ZN = 4
 XN = 4
 QCAP = 4
+START = ("s0", "m2", "s1", "m3")
+LOOK = {2: ("x0",), 5: ("x1", "s2", "m4")}
+MIDDLE = ("o0", "s3", "m5", "x2", "o1")
+LATER = ("s4", "m6", "x3", "o2", "s5", "m7", "x4", "o3")
+LAST = ("s6", "x5", "o4")
+LOOP = {(0, 0): ("s7", "x6", "o5"), (1, 0): ("x7", "o6"), (2, 0): ("o7",)}
 BF = jnp.bfloat16
 F32 = jnp.float32
 I32 = jnp.int32
@@ -37,7 +43,7 @@
     cache_ref, wqu_ref, wout_ref, table, sendbuf, inc0, inc1, inc2, inc3, inc4, inc5, inc6, inc7, migbuf, split, parted, kv,
     meta_own, meta, ns_vec, ns_smem, len_vec,
     ids_pad, inv_pad, req_own, req1, req2, req3, col, acc, resp, back, turned, fetched,
-    turn, pick, csend, cand, query, gate, mixed, ssend, sback,
+    turn, fold_ref, pick, csend, cand, query, gate, mixed, ssend, sback,
     cache_sem, wqu_sem, wout_sem, table_sem, small_sem, out_sem,
     meta_s, meta_r, m_s, m_r, z_s, z_r, x_s, x_r, f_s, f_r,
     q1_s, q1_r, q2_s, q2_r, p1_s, p1_r, p2_s, p2_r, c_s, c_r, o_s, o_r,
@@ -202,9 +208,6 @@
 
     def settle(e):
         wait_bytes(incoming[e].at[pl.ds(0, 7)], m_r.at[e])
-        if e + AHEAD < CHUNKS:
-            prepare(e + AHEAD)
-            each(1, 8, lambda d: migrate(e + AHEAD, d).start())
         for k in range(4):
             rows = incoming[e][sources[k]]
             migbuf[e, k] = rows
@@ -229,6 +232,15 @@
     def store_out(e):
         return pltpu.make_async_copy(migbuf.at[e], mig_out.at[:, pl.ds(e * block, block), :], out_sem)
 
+    def launch(e):
+        if e >= AHEAD:
+            prepare(e)
+        each(1, 8, lambda d: migrate(e, d).start())
+
+    def steps(names):
+        for name in names:
+            {"m": launch, "s": settle, "x": spread, "o": onward}[name[0]](int(name[1:]))
+
     load_cache.wait()
     for e in range(AHEAD):
         prepare(e)
@@ -236,7 +248,7 @@
     each(1, 8, lambda d: request_s(d).start())
     each(1, 8, lambda d: tell(d).start())
     for e in range(AHEAD):
-        each(1, 8, functools.partial(lambda e, d: migrate(e, d).start(), e))
+        launch(e)
     own = pl.ds(pl.multiple_of(sess * 16, 16), 16)
     req1[own] = req_own[own]
 
@@ -283,9 +295,7 @@
 
     sources = [source(k) for k in range(4)]
 
-    settle(0)
-    settle(1)
-
+    steps(START)
     wait_bytes(req3.at[pl.ds(0, 15)], q2_r)
     for i in range(16):
         asked = req3[i]
@@ -303,11 +313,8 @@
         acc[...] += dot(hot, table[pl.ds(pl.multiple_of(base, depth), depth), :])
 
     def look_ups(c):
-        @pl.when(c == items // depth // 2)
-        def _():
-            spread(0)
-            spread(1)
-
+        for slot, names in LOOK.items():
+            pl.when(c == slot)(functools.partial(steps, names))
         look_up(c)
 
     each(0, items // depth, look_ups)
@@ -316,23 +323,14 @@
     back[item] = resp[item]
     each(1, 16, lambda d: response_i(d).start())
 
-    settle(2)
-    onward(0)
-    settle(3)
-    onward(1)
-    spread(2)
+    steps(MIDDLE)
 
     wait_bytes(back.at[pl.ds(0, 15)], p1_r)
     turned[...] = dot(turn[...], back[...].reshape(512, width)).astype(BF).reshape(8, 64, width)
     fetched[sess] = turned[sess]
     each(1, 8, lambda d: response_s(d).start())
 
-    settle(4)
-    spread(3)
-    onward(2)
-    settle(5)
-    spread(4)
-    onward(3)
+    steps(LATER)
 
     wait_bytes(fetched.at[pl.ds(0, 7)], p2_r)
 
@@ -344,12 +342,7 @@
         send_cand(g).start()
     cand[0] = make_cand(0)
 
-    settle(6)
-    spread(5)
-    onward(4)
-    settle(7)
-    spread(6)
-    onward(5)
+    steps(LAST)
 
     load_wqu.wait()
 
@@ -363,17 +356,30 @@
     wait_bytes(cand.at[pl.ds(1, 3)], c_r)
     each(0, 4, project)
 
+    load_wout.wait()
+    head = jnp.broadcast_to(whead_ref[...].astype(F32).reshape(1, width), (16, width)).astype(BF)
+    fold = dot_nt(head, wout_ref[...])
+    fold0 = fold.astype(BF)
+    left = fold - fold0.astype(F32)
+    fold1 = left.astype(BF)
+    fold2 = (left - fold1.astype(F32)).astype(BF)
+    which_row = iota((16, width), 0)
+    folds = jnp.where(
+        which_row == 0, fold0.astype(F32),
+        jnp.where(which_row == 1, fold1.astype(F32), jnp.where(which_row == 2, fold2.astype(F32), 0.0))).astype(BF)
+    fold_ref[0] = folds
+    fold_ref[1] = jnp.where(which_row == 0, head.astype(F32), 0.0).astype(BF)
+
+    def finish(r):
+        m = mixed[r]
+        normed = m * lax.rsqrt(jnp.mean(m * m, axis=1, keepdims=True) + 1e-6)
+        gated = (normed * gate[r]).astype(BF)
+        part = dot_nt(fold_ref[0], gated) + dot_nt(fold_ref[1], cand[r])
+        line = jnp.sum(part, axis=0, keepdims=True)
+        ssend[r] = jnp.broadcast_to(line, (8, count))
+
     def attend(p):
         e = 2 * p
-
-        @pl.when(p == 1)
-        def _():
-            spread(7)
-            onward(6)
-
-        @pl.when(p == 2)
-        def _():
-            onward(7)
 
         arrive(e)
         arrive(e + 1)
@@ -403,37 +409,23 @@
                     total = total + dot(w, values)
                 mixed[r, :, cols] = total
 
-        each(0, 4, rows)
+        def turns(n):
+            for (slot_p, slot_n), names in LOOP.items():
+                pl.when((p == slot_p) & (n == slot_n))(functools.partial(steps, names))
+            r = lax.rem(n + 1, 4)
+            rows(r)
+
+            @pl.when(p == CHUNKS // 2 - 1)
+            def _():
+                finish(r)
+
+                @pl.when(r != 0)
+                def _():
+                    send_score(r).start()
+
+        each(0, 4, turns)
 
     each(0, CHUNKS // 2, attend)
-
-    load_wout.wait()
-    head = jnp.broadcast_to(whead_ref[...].astype(F32).reshape(1, width), (16, width)).astype(BF)
-    fold = dot_nt(head, wout_ref[...])
-    fold0 = fold.astype(BF)
-    left = fold - fold0.astype(F32)
-    fold1 = left.astype(BF)
-    fold2 = (left - fold1.astype(F32)).astype(BF)
-    which_row = iota((16, width), 0)
-    folds = jnp.where(
-        which_row == 0, fold0.astype(F32),
-        jnp.where(which_row == 1, fold1.astype(F32), jnp.where(which_row == 2, fold2.astype(F32), 0.0))).astype(BF)
-    heads = jnp.where(which_row == 0, head.astype(F32), 0.0).astype(BF)
-
-    def finish(r):
-        m = mixed[r]
-        normed = m * lax.rsqrt(jnp.mean(m * m, axis=1, keepdims=True) + 1e-6)
-        gated = (normed * gate[r]).astype(BF)
-        part = dot_nt(folds, gated) + dot_nt(heads, cand[r])
-        line = jnp.sum(part, axis=0, keepdims=True)
-        ssend[r] = jnp.broadcast_to(line, (8, count))
-
-    def finish_send(g):
-        finish(g)
-        send_score(g).start()
-
-    each(1, 4, finish_send)
-    finish(0)
     sback[0] = ssend[0]
 
     wait_bytes(req_own.at[pl.ds(0, 112)], q1_s)
@@ -519,6 +511,7 @@
         pltpu.VMEM((8, 64, width), BF),
         pltpu.VMEM((8, 64, width), BF),
         pltpu.VMEM((512, 512), BF),
+        pltpu.VMEM((2, 16, width), BF),
         pltpu.VMEM((4, count, 512), BF),
         pltpu.VMEM((4, count, width), BF),
         pltpu.VMEM((4, count, width), BF),

time: 110 us -> 107 us (0.973)
  Pallas kernels: 110 us -> 106 us
    pallas_call x1, Pallas kernels: 106 us -> 103 us  [per_device(): pl.pallas_call(kernel, out_shape=(jax.ShapeDtypeStruct(whole.shape, BF),...]
where the time goes in v3:
time: 107 us
  Pallas kernels  106 us (99%)
    pallas_call x1, Pallas kernels, per_device(): pl.pallas_call(kernel, out_shape=(jax.ShapeDtypeStruct(whole.shape, BF),...  103 us
    pallas_call x1, Pallas kernels, per_device(): pl.pallas_call(hand_on, out_shape=(jax.ShapeDtypeStruct(whole.shape, BF),...  3.84 us

profile of v3, /device:TPU:0, one launch (start us, length us, event | category | flops | bytes accessed | tf_op | source)
XLA Modules:
  0.0 107.0 jit_solution(9040565525922372087)
XLA Ops:
  0.6 102.5 %shard_map.104 = (bf16[4,2048,128]{2,1,0:T(8,128)(2,1)}, f32[4,256]{1,0:T(4,128)}) custom-call(s32[4]{0:T(128)} %ns_ref.1, s32[4]{0:T(128)} %ln_ref.1, s32[1,320]{1,0:T(1,128)} %ids_ref.1, s32[4,256]{1,0:T(4,128)} %inv_ref.1, bf16[4,2048,128]{2,1,0:T(8,128)(2,1)} %bitcast.10, bf16[8192,512]{1,0:T(8,128)(2,1)} %table_ref.1, bf16[512,1024]{1,0:T(8,128)(2,1)} %wqu_hbm.1, ...), custom_call_target="tpu_custom_call" | custom-call | flops 12000000000 | bytes 16000000 | tf_op jit(solution)/shard_map/pallas_call | solution.py:533
  103.2 3.8 %shard_map.105 = (bf16[4,2048,128]{2,1,0:T(8,128)(2,1)}, f32[4,256]{1,0:T(4,128)}) custom-call(bf16[4,2048,128]{2,1,0:T(8,128)(2,1)} %get-tuple-element.6.mig_ref, f32[4,256]{1,0:T(4,128)} %get-tuple-element.7.score_ref), custom_call_target="tpu_custom_call" | custom-call | tf_op jit(solution)/shard_map/pallas_call | solution.py:546

commit v4 on v3

--- a/solution.py
+++ b/solution.py
@@ -353,8 +353,7 @@
         gate[r] = g / (1.0 + jnp.exp(-g))
         mixed[r] = jnp.zeros(mixed.shape[1:], F32)
 
-    wait_bytes(cand.at[pl.ds(1, 3)], c_r)
-    each(0, 4, project)
+    project(0)
 
     load_wout.wait()
     head = jnp.broadcast_to(whead_ref[...].astype(F32).reshape(1, width), (16, width)).astype(BF)
@@ -369,6 +368,10 @@
         jnp.where(which_row == 1, fold1.astype(F32), jnp.where(which_row == 2, fold2.astype(F32), 0.0))).astype(BF)
     fold_ref[0] = folds
     fold_ref[1] = jnp.where(which_row == 0, head.astype(F32), 0.0).astype(BF)
+
+    wait_bytes(cand.at[pl.ds(1, 3)], c_r)
+    each(1, 4, project)
+
 
     def finish(r):
         m = mixed[r]

time: 107 us -> 107 us (level)
  no operation moved by 1% of the time
where the time goes in v4:
time: 107 us
  Pallas kernels  106 us (99%)
    pallas_call x1, Pallas kernels, per_device(): pl.pallas_call(kernel, out_shape=(jax.ShapeDtypeStruct(whole.shape, BF),...  102 us
    pallas_call x1, Pallas kernels, per_device(): pl.pallas_call(hand_on, out_shape=(jax.ShapeDtypeStruct(whole.shape, BF),...  3.84 us

profile of v4, /device:TPU:0, one launch (start us, length us, event | category | flops | bytes accessed | tf_op | source)
XLA Modules:
  0.0 106.5 jit_solution(12067761182994773808)
XLA Ops:
  0.6 102.0 %shard_map.104 = (bf16[4,2048,128]{2,1,0:T(8,128)(2,1)}, f32[4,256]{1,0:T(4,128)}) custom-call(s32[4]{0:T(128)} %ns_ref.1, s32[4]{0:T(128)} %ln_ref.1, s32[1,320]{1,0:T(1,128)} %ids_ref.1, s32[4,256]{1,0:T(4,128)} %inv_ref.1, bf16[4,2048,128]{2,1,0:T(8,128)(2,1)} %bitcast.10, bf16[8192,512]{1,0:T(8,128)(2,1)} %table_ref.1, bf16[512,1024]{1,0:T(8,128)(2,1)} %wqu_hbm.1, ...), custom_call_target="tpu_custom_call" | custom-call | flops 12000000000 | bytes 16000000 | tf_op jit(solution)/shard_map/pallas_call | solution.py:536
  102.7 3.8 %shard_map.105 = (bf16[4,2048,128]{2,1,0:T(8,128)(2,1)}, f32[4,256]{1,0:T(4,128)}) custom-call(bf16[4,2048,128]{2,1,0:T(8,128)(2,1)} %get-tuple-element.6.mig_ref, f32[4,256]{1,0:T(4,128)} %get-tuple-element.7.score_ref), custom_call_target="tpu_custom_call" | custom-call | tf_op jit(solution)/shard_map/pallas_call | solution.py:549
